TPU v7x, 1024 devices: a whole 4x8x16 slice. The times are simulated.
1024 devices in a mesh: pool: 8 (over y_lo, x), peer: 32 (over z, core), sub: 4 (over y_hi).
Axes of the slice: x: 4, y: 8 (y_hi: 4, y_lo: 2; y = y_hi * 2 + y_lo), z: 16, core: 2. Of those that a mesh axis runs over, the one named last changes fastest.
Arguments:
- x_a: bfloat16 [2048, 7168], P(('peer', 'sub'), 'pool'), may hold values from -6 to 6
- routes: int32 [2048, 8], P(('peer', 'sub')), may hold values from 0 to 31, all different within a row; in each aligned block of 16 rows (0 to 15, 16 to 31, ...) at most 5 rows name the same one
- route_score: float32 [2048, 8], P(('peer', 'sub')), may hold values from 0.05 to 1
- w_gate: bfloat16 [32, 7168, 2048], P('peer', 'pool', 'sub'), may hold values from -0.0625 to 0.0625
- w_up: bfloat16 [32, 7168, 2048], P('peer', 'pool', 'sub'), may hold values from -0.0625 to 0.0625
- w_down: bfloat16 [32, 2048, 7168], P('peer', 'sub', 'pool'), may hold values from -0.125 to 0.125
- queries: bfloat16 [1024, 128, 576], P(('pool', 'peer', 'sub')), may hold values from -64 to 64
- cache: bfloat16 [1024, 128, 576], P(('pool', 'peer', 'sub')), may hold values from -4 to 4
- lengths: int32 [1024], P(('pool', 'peer', 'sub')), may hold values from 1 to 128, as said below
Outputs:
- moe_out: bfloat16 [2048, 7168], P(('peer', 'sub'), 'pool')
- context: bfloat16 [1024, 128, 512], P(('pool', 'peer', 'sub'))
Inputs may be any that keep to these rules, and one draw needn't show every extreme that they name: `routes`: each row names 8 different experts; within the rows of one device no expert is named more than 5 times. `lengths`: request 0 uses the whole cache.
All inputs are finite; a program needn't handle non-finite values.
Results may differ from a plain program's by a relative error of at most 0.011.
Values may be sent and summed in bfloat16 or wider, within the bound.
A program may use at most 32 MiB of HBM per device.

v0:
```python
import jax
import jax.numpy as jnp
from jax import lax
from jax.sharding import PartitionSpec as P

KV_RANK = 512
ROPE_DIM = 64
NOPE_DIM = 128


routed_scaling = 2.5


def per_device(x_a, routes, route_score, w_gate, w_up, w_down, queries, cache, lengths):
    peers = lax.axis_size("peer")
    per_peer = w_gate.shape[0]
    experts = per_peer * peers
    tok_count = routes.shape[0]
    choose = routes.shape[1]
    depth = tok_count * choose // experts + 1
    width_local = x_a.shape[1]
    highest_prec = lax.Precision.HIGHEST
    flat_ids = routes.reshape(-1)
    expert_hit = (flat_ids[:, None] == jnp.arange(experts, dtype=jnp.int32)[None, :]).astype(
        jnp.int32
    )
    earlier = jnp.cumsum(expert_hit, axis=0) - expert_hit
    slot_index = jnp.sum(earlier * expert_hit, axis=1)
    target = flat_ids * depth + slot_index
    placed = (target[:, None] == jnp.arange(experts * depth, dtype=jnp.int32)[None, :]).astype(
        jnp.float32
    )
    token_of = jnp.arange(tok_count * choose, dtype=jnp.int32) // choose
    owner = (token_of[:, None] == jnp.arange(tok_count, dtype=jnp.int32)[None, :]).astype(
        jnp.float32
    )
    selector = jnp.dot(placed.T, owner, precision=highest_prec).astype(jnp.bfloat16)
    outgoing = jnp.dot(selector, x_a, preferred_element_type=jnp.float32).astype(jnp.bfloat16)
    outgoing = outgoing.reshape(peers, per_peer * depth, width_local)
    grouped = lax.all_gather(outgoing[None], "sub", axis=0, tiled=True)
    arrived = lax.all_to_all(grouped, "peer", split_axis=1, concat_axis=1, tiled=True)
    subs = arrived.shape[0]
    stacked = arrived.reshape(subs * peers, per_peer, depth, width_local)
    gate_part = jnp.einsum("rlmd,ldf->rlmf", stacked, w_gate, preferred_element_type=jnp.float32)
    upper_part = jnp.einsum("rlmd,ldf->rlmf", stacked, w_up, preferred_element_type=jnp.float32)
    gate_full, upper_full = lax.psum((gate_part, upper_part), "pool")
    hidden = (jax.nn.silu(gate_full) * upper_full).astype(jnp.bfloat16)
    partial_out = jnp.einsum("rlmf,lfd->rlmd", hidden, w_down, preferred_element_type=jnp.float32)
    partial_out = partial_out.reshape(subs, peers, per_peer * depth, width_local)
    returned = lax.all_to_all(partial_out, "peer", split_axis=1, concat_axis=1, tiled=True)
    summed = lax.psum_scatter(returned, "sub", scatter_dimension=0, tiled=True)
    expert_out = summed[0].astype(jnp.bfloat16)
    results = expert_out.reshape(experts * depth, width_local).astype(jnp.float32)
    weights = routed_scaling * route_score / jnp.sum(route_score, axis=1, keepdims=True)
    mixing = jnp.dot(owner.T, placed * weights.reshape(-1)[:, None], precision=highest_prec)
    moe_out = jnp.dot(mixing, results, precision=highest_prec).astype(jnp.bfloat16)
    scale = (NOPE_DIM + ROPE_DIM) ** (-0.5)
    span = cache.shape[1]
    scores = jnp.einsum("thc,tlc->thl", queries, cache, preferred_element_type=jnp.float32) * scale
    valid = jnp.arange(span, dtype=jnp.int32)[None, None, :] < lengths[:, None, None]
    top_score = jnp.max(jnp.where(valid, scores, -jnp.inf), axis=2, keepdims=True)
    expo = jnp.where(valid, jnp.exp(scores - top_score), 0.0)
    probs = (expo / jnp.sum(expo, axis=2, keepdims=True)).astype(jnp.bfloat16)
    context = jnp.einsum(
        "thl,tlc->thc", probs, cache[:, :, :KV_RANK], preferred_element_type=jnp.float32
    )
    return (moe_out, context.astype(jnp.bfloat16))


def solution(mesh):
    placed = (
        P(("peer", "sub"), "pool"),
        P(("peer", "sub"), None),
        P(("peer", "sub"), None),
        P("peer", "pool", "sub"),
        P("peer", "pool", "sub"),
        P("peer", "sub", "pool"),
        P(("pool", "peer", "sub"), None, None),
        P(("pool", "peer", "sub"), None, None),
        P(("pool", "peer", "sub")),
    )
    return jax.shard_map(
        per_device,
        mesh=mesh,
        in_specs=placed,
        out_specs=(P(("peer", "sub"), "pool"), P(("pool", "peer", "sub"), None, None)),
        check_vma=False,
    )
```

profile of v0, /device:TPU:6, one launch (start us, length us, event | category | flops | bytes accessed | tf_op | source)
XLA Modules:
  0.0 427.2 jit_solution(11421949003246290074)
XLA Ops:
  7.2 0.0 copy-start
  7.2 0.0 all-gather.2.cloned.1.call-start
  7.2 0.8 copy.24
  8.1 0.1 reshape.100
  8.1 0.1 fusion.16
  8.2 0.2 reduce_window_sum.11
  8.4 0.2 select_reduce_fusion.1
  8.6 0.3 convolution_convert_fusion.3
  8.9 1.0 convolution_convert_fusion
  9.9 0.1 broadcast_in_dim_reshape.2
  10.0 0.7 copy.26
  10.7 0.0 all-gather.2.cloned.1.call-update
  10.8 0.0 all-reduce.3.cloned.1.call-start
  10.8 52.1 %all-gather.2.cloned.1.call-done = bf16[4,32,5,896]{3,1,2,0:T(8,128)(2,1)} async-done(((bf16[1,32,5,896]{3,1,2,0:T(8,128)(2,1)}), bf16[4,32,5,896]{3,1,2,0:T(8,128)(2,1)}) %all-gather.2.cloned.1.call-update) | async-done | bytes 1146896 | tf_op jit(solution)/shard_map/all_gather | solution.py:40
  62.9 1.8 copy.27
  64.8 73.8 %all_to_all.10 = bf16[4,32,5,896]{3,0,2,1:T(4,128)(2,1)S(1)} all-to-all(bf16[4,32,5,896]{3,0,2,1:T(4,128)(2,1)S(1)} %copy.27), channel_id=1, replica_groups=mesh['pool'=8,'peer'=32,'sub'=4] {'peer'}, dimensions={1} | all-to-all | bytes 2293760 | tf_op jit(solution)/shard_map/all_to_all | solution.py:41
  138.6 0.0 copy-start.4
  138.6 0.1 copy.28
  138.8 1.0 copy-done.4
  139.8 0.0 copy-start.5
  139.8 1.9 convolution_bitcast_fusion
  141.7 0.0 copy-done.5
  141.7 1.9 convolution_bitcast_fusion.1
  143.7 0.0 all-reduce.3.cloned.1.call-update
  143.7 0.0 reduce-scatter.2.cloned.1.call-start
  143.7 93.9 %all-reduce.3.cloned.1.call-done = (f32[128,1,5,512]{3,0,2,1:T(8,128)}, f32[128,1,5,512]{3,0,2,1:T(8,128)}) async-done(((f32[128,1,5,512]{3,0,2,1:T(8,128)}, f32[128,1,5,512]{3,0,2,1:T(8,128)}), (f32[128,1,5,512]{3,0,2,1:T(8,128)}, f32[128,1,5,512]{3,0,2,1:T(8,128)})) %all-reduce.3.cloned.1.call-update) | async-done | bytes 2621456 | tf_op jit(solution)/shard_map/psum | solution.py:46
  237.6 0.0 copy-done
  237.6 2.6 fusion.1
  240.2 1.5 copy.29
  241.7 123.0 %all_to_all.11 = f32[4,32,5,896]{3,0,2,1:T(4,128)S(1)} all-to-all(f32[4,32,5,896]{3,0,2,1:T(4,128)S(1)} %copy.29), channel_id=1, replica_groups=mesh['pool'=8,'peer'=32,'sub'=4] {'peer'}, dimensions={1} | all-to-all | bytes 4587520 | tf_op jit(solution)/shard_map/all_to_all | solution.py:50
  364.6 1.7 copy.30
  366.3 0.0 copy-start.3
  366.3 0.0 copy-start.1
  366.3 0.0 copy-start.2
  366.3 0.0 reduce-scatter.2.cloned.1.call-update
  366.3 0.7 copy-done.3
  367.0 0.1 copy.25
  367.1 0.1 mul.48
  367.9 0.0 copy-done.1
  367.9 0.0 copy-done.2
  367.9 0.3 select_reduce_fusion
  368.2 0.1 fusion.17
  368.3 0.9 fusion
  369.2 0.3 fusion.10
  369.5 49.0 %reduce-scatter.2.cloned.1.call-done = f32[1,32,5,896]{3,1,2,0:T(8,128)} async-done(((f32[4,32,5,896]{3,1,2,0:T(8,128)}), f32[1,32,5,896]{3,1,2,0:T(8,128)}) %reduce-scatter.2.cloned.1.call-update) | async-done | bytes 573456 | tf_op jit(solution)/shard_map/reduce_scatter | solution.py:51
  418.5 1.1 convert_element_type.39
  419.6 0.1 copy.31
  419.7 0.1 convert_element_type.40
  419.9 0.9 convolution_convert_fusion.2
  (4 shorter events, 0.0 us)
Async XLA Ops:
  7.2 230.4 %copy-start = (bf16[1,512,896]{2,1,0:T(8,128)(2,1)S(1)}, bf16[1,512,896]{2,1,0:T(8,128)(2,1)}, u32[]{:S(2)}) copy-start(bf16[1,512,896]{2,1,0:T(8,128)(2,1)} %param.14) | copy-start | bytes 2752516
  7.2 55.8 %all-gather.2.cloned.1.call-start = ((), (), s32[]{:S(2)}) async-start(), calls=%async_computation.3 | async-start | bytes 1433600 | tf_op jit(solution)/shard_map/all_gather | solution.py:40
  10.8 226.8 %all-reduce.3.cloned.1.call-start = ((), (), s32[]{:S(2)}) async-start(), calls=%async_computation.5 | async-start | bytes 5242880 | tf_op jit(solution)/shard_map/psum | solution.py:46
  138.6 1.2 copy-start.4
  139.8 1.9 copy-start.5
  143.7 274.8 %reduce-scatter.2.cloned.1.call-start = ((), (), s32[]{:S(2)}) async-start(), calls=%async_computation.4 | async-start | bytes 2867200 | tf_op jit(solution)/shard_map/reduce_scatter | solution.py:51
  366.3 0.7 copy-start.3
  366.3 1.6 copy-start.1
  366.3 1.6 copy-start.2
Sparse Core Ops, SparseCore 0:
  10.9 52.0 all-gather.1
  143.8 93.7 all-reduce.2
  366.5 52.0 reduce-scatter.1
where the time goes:
time: 428 us; the launch traced here: 427 us
  blocking collectives  197 us (46%)
  waiting for transfers between devices  195 us (46%)
  between operations  14.5 us (3%)
  matrix products  10.1 us (2%)
  local copies, waits for them, and re-layouts  9.02 us (2%)
    all_to_all x1, blocking collectives, per_device(): lax.all_to_all(partial_out, 'peer', split_axis=1, concat_axis=1, tiled=True)  123 us
    psum x1, waiting for transfers between devices, per_device(): gate_full, upper_full = lax.psum((gate_part, upper_part), 'pool')  93.9 us
    all_to_all x1, blocking collectives, per_device(): lax.all_to_all(grouped, 'peer', split_axis=1, concat_axis=1, tiled=True)  73.8 us
    all_gather x1, waiting for transfers between devices, per_device(): grouped = lax.all_gather(outgoing[None], 'sub', axis=0, tiled=True)  52.1 us
    reduce_scatter x1, waiting for transfers between devices, per_device(): summed = lax.psum_scatter(returned, 'sub', scatter_dimension=0, tiled=True)  49 us
  transfers between devices with their start and end apart: 3, of which 3 were waited for; matrix products, arithmetic and copies ran while one was open for 0% of the time, Pallas kernels for 0%

commit v1 on v0

v1 whole, which is shorter than its diff:
```python
import functools

import jax
import jax.numpy as jnp
from jax import lax
from jax.experimental import pallas as pl
from jax.experimental.pallas import tpu as pltpu
from jax.sharding import PartitionSpec as P

KV_RANK = 512
SCALE = 192 ** (-0.5)
ROUTED = 2.5
TOK = 16
MOST = 5
WIDTH = 896
WIDE = 1024
FFS = 512
GROUP = 16 * MOST
SHARE = FFS // 4
MESH = pl.DeviceIdType.MESH
F32, BF16 = jnp.float32, jnp.bfloat16


def kernel(
    x_ref, routes_ref, score_ref, len_ref, wg_hbm, wu_hbm, wd_hbm, q_hbm, c_hbm,
    moe_ref, ctx_hbm,
    xb, wg, wu, wd, qv, cv, ctxv, sp, rp, hr, co, cs, cm, zs, zr, fs, yr,
    load_sem, y_send, y_recv, ring_send, ring_recv, mate_send, mate_recv,
    rp_send, rp_recv, h_send, h_recv, cm_send, cm_recv, z_send, z_recv, f_send, f_recv,
):
    pool, peer, sub = lax.axis_index("pool"), lax.axis_index("peer"), lax.axis_index("sub")
    row, col = pool // 4, lax.rem(pool, 4)
    up_dev = {"peer": lax.rem(peer + 2, 32)}
    down_dev = {"peer": lax.rem(peer + 30, 32)}
    mate_dev = {"peer": peer + 1 - 2 * lax.rem(peer, 2)}

    def sub_dev(d):
        return {"sub": lax.rem(sub + d, 4)}

    def pool_dev(d):
        return {"pool": lax.rem(pool + d, 8)}

    def send(src, dst, ssem, rsem, dev):
        pltpu.make_async_remote_copy(
            src_ref=src, dst_ref=dst, send_sem=ssem, recv_sem=rsem,
            device_id=dev, device_id_type=MESH,
        ).start()

    def wait(ref, sem):
        pltpu.make_async_copy(ref, ref, sem).wait()

    barrier = pltpu.get_barrier_semaphore()
    partners = [up_dev, down_dev, mate_dev]
    partners += [sub_dev(d) for d in range(1, 4)] + [pool_dev(d) for d in range(1, 8)]
    for dev in partners:
        pl.semaphore_signal(barrier, inc=1, device_id=dev, device_id_type=MESH)

    loads = [
        pltpu.make_async_copy(src, dst, load_sem.at[n])
        for n, (src, dst) in enumerate(
            ((q_hbm.at[0], qv), (c_hbm.at[0], cv), (wg_hbm.at[0], wg), (wu_hbm.at[0], wu), (wd_hbm.at[0], wd))
        )
    ]
    for load in loads:
        load.start()

    lane = lax.broadcasted_iota(jnp.int32, (TOK, 128), 1)
    score = score_ref[...]
    weight = ROUTED * score / jnp.sum(score, axis=1, keepdims=True)
    hit = jnp.zeros((TOK, 128), F32)
    mix = jnp.zeros((TOK, 128), F32)
    for k in range(8):
        expert = routes_ref[:, k : k + 1]
        w = weight[:, k : k + 1]
        high = w.astype(BF16).astype(F32)
        hit = hit + jnp.where(lane == expert, 1.0, 0.0)
        mix = mix + jnp.where(lane == expert + 32, high, 0.0)
        mix = mix + jnp.where(lane == expert + 64, w - high, 0.0)
    before = (
        lax.broadcasted_iota(jnp.int32, (TOK, TOK), 1) < lax.broadcasted_iota(jnp.int32, (TOK, TOK), 0)
    )
    earlier = jnp.dot(jnp.where(before, 1.0, 0.0).astype(BF16), hit.astype(BF16), preferred_element_type=F32)
    table = (earlier + 1.0) * hit + mix
    xb[0, 0, 0, 0:TOK, 0:WIDTH] = x_ref[...]
    xb[0, 0, 0, 0:TOK, WIDTH:WIDE] = table.astype(BF16)

    pl.semaphore_wait(barrier, len(partners))

    def rows(i):
        return pl.ds(TOK * i, TOK)

    def pass_up(a, i):
        send(xb.at[0, a, 0, rows(i)], xb.at[0, a + 1, 0, rows(i)], ring_send, ring_recv.at[0, a + 1, i], up_dev)

    def pass_down(a, i):
        send(xb.at[1, a, 0, rows(i)], xb.at[1, a + 1, 0, rows(i)], ring_send, ring_recv.at[1, a + 1, i], down_dev)

    def to_mate(h, a):
        send(xb.at[h, a, 0], xb.at[h, a, 1], mate_send, mate_recv.at[h, a], mate_dev)

    for d in (2, 1, 3):
        send(xb.at[0, 0, 0, rows(0)], xb.at[0, 0, 0, rows(4 - d)], y_send, y_recv.at[4 - d], sub_dev(d))
    for i in (0, 1, 3, 2):
        if i:
            wait(xb.at[0, 0, 0, rows(i)], y_recv.at[i])
        pass_up(0, i)
        send(xb.at[0, 0, 0, rows(i)], xb.at[1, 0, 0, rows(i)], ring_send, ring_recv.at[1, 0, i], down_dev)
    to_mate(0, 0)

    loads[0].wait()
    loads[1].wait()
    entries = cv[...]
    scores = lax.dot_general(qv[...], entries, (((1,), (1,)), ((), ())), preferred_element_type=F32) * SCALE
    valid = lax.broadcasted_iota(jnp.int32, scores.shape, 1) < len_ref[...]
    top = jnp.max(jnp.where(valid, scores, -jnp.inf), axis=1, keepdims=True)
    expo = jnp.where(valid, jnp.exp(scores - top), 0.0)
    probs = (expo / jnp.sum(expo, axis=1, keepdims=True)).astype(BF16)
    ctxv[...] = jnp.dot(probs, entries[:, 0:KV_RANK], preferred_element_type=F32).astype(BF16)
    ctx_out = pltpu.make_async_copy(ctxv, ctx_hbm.at[0], load_sem.at[5])
    ctx_out.start()
    for load in loads[2:]:
        load.wait()

    def placing(h, u):
        tab = xb[h, pl.ds(2 * u, 2), :, :, WIDTH:WIDE].reshape(256, 128).astype(F32)
        lanes = lax.broadcasted_iota(jnp.int32, (256, 128), 1)
        slot = jnp.sum(jnp.where(lanes == peer, tab, 0.0), axis=1, keepdims=True)
        share = jnp.where((lanes == peer + 32) | (lanes == peer + 64), tab, 0.0)
        wt = jnp.sum(share, axis=1, keepdims=True)
        base = lax.broadcasted_iota(jnp.int32, (256, 1), 0) // TOK * MOST - 1
        place = jnp.where(slot > 0.5, slot.astype(jnp.int32) + base, -1)
        onehot = lax.broadcasted_iota(jnp.int32, (256, GROUP), 1) == place
        return jnp.where(onehot, 1.0, 0.0).astype(BF16), wt

    def gates(k):
        u, h = k // 2, lax.rem(k, 2)
        for j in range(2):
            wait(xb.at[h, 2 * u + j, 1], mate_recv.at[h, 2 * u + j])
        onehot, _ = placing(h, u)
        x = xb[h, pl.ds(2 * u, 2), :, :, 0:WIDTH].reshape(256, WIDTH)
        picked = lax.dot_general(onehot, x, (((0,), (0,)), ((), ())), preferred_element_type=F32).astype(BF16)
        gate = jnp.dot(picked, wg[...], preferred_element_type=F32).astype(BF16)
        for n in range(4):
            sp[k, n, :, 0:SHARE] = gate[:, SHARE * n : SHARE * (n + 1)]
        upper = jnp.dot(picked, wu[...], preferred_element_type=F32).astype(BF16)
        for n in range(4):
            sp[k, n, :, SHARE : 2 * SHARE] = upper[:, SHARE * n : SHARE * (n + 1)]

        def give(d):
            c = lax.rem(col + d, 4)
            dest = h * 4 + c
            place = lax.rem(pool - dest + 8, 8) - 1
            send(sp.at[k, c], rp.at[u, place], rp_send, rp_recv.at[u], {"pool": dest})

        for d in (2, 1, 3):
            give(d)

        @pl.when(h != row)
        def _():
            give(0)

    def hidden(u):
        wait(rp.at[u], rp_recv.at[u])
        total = sp[2 * u + row, col].astype(F32)
        for n in range(7):
            total = total + rp[u, n].astype(F32)
        gate, upper = total[:, 0:SHARE], total[:, SHARE : 2 * SHARE]
        hr[u, pool] = (gate / (1.0 + jnp.exp(-gate)) * upper).astype(BF16)
        for d in (6, 2, 5, 7, 3, 1, 4):
            send(hr.at[u, pool], hr.at[u, pool], h_send, h_recv.at[u], pool_dev(d))

    def down(u):
        wait(hr.at[u, 0:7], h_recv.at[u])
        for h in range(2):
            hid = jnp.concatenate([hr[u, 4 * h + n] for n in range(4)], axis=1)
            out = jnp.dot(hid, wd[...], preferred_element_type=F32).astype(BF16)
            onehot, wt = placing(h, u)
            mixed = wt * jnp.dot(onehot, out, preferred_element_type=F32)
            for j in range(2):
                a = 2 * u + j
                cs[h, a] = mixed[128 * j + 64 : 128 * j + 128].astype(BF16)
                send(cs.at[h, a], cm.at[h, a], cm_send, cm_recv.at[h, a], mate_dev)
                co[h, a] = mixed[128 * j : 128 * j + 64]

    def hop(t, _):
        @pl.when(t <= 8)
        def _():
            for i in (0, 1, 3, 2):
                @pl.when(t <= 7)
                def _():
                    wait(xb.at[0, t, 0, rows(i)], ring_recv.at[0, t, i])

                @pl.when(t <= 6)
                def _():
                    pass_up(t, i)

                wait(xb.at[1, t - 1, 0, rows(i)], ring_recv.at[1, t - 1, i])

                @pl.when(t <= 7)
                def _():
                    pass_down(t - 1, i)

            @pl.when(t <= 7)
            def _():
                to_mate(0, t)

            to_mate(1, t - 1)

        @pl.when(t >= 2)
        def _():
            gates(t - 2)

        @pl.when((t >= 5) & (lax.rem(t, 2) == 1))
        def _():
            hidden((t - 5) // 2)

        @pl.when((t >= 7) & (lax.rem(t, 2) == 1))
        def _():
            down((t - 7) // 2)

        return 0

    lax.fori_loop(1, 10, hop, 0)
    hidden(3)
    down(2)
    down(3)

    def own(h, a, i):
        return co[h, a, rows(i)] + cm[h, a, rows(i)].astype(F32)

    def back(h, a, i, dev):
        after = lax.rem(a + 7, 8)
        send(zs.at[h, a, rows(i)], zr.at[h, after, rows(i)], z_send, z_recv.at[h, after, i], dev)

    ways = ((0, down_dev), (1, up_dev))
    order = (2, 1, 3, 0)
    for h, dev in ways:
        wait(cm.at[h, 7], cm_recv.at[h, 7])
    for i in order:
        for h, dev in ways:
            zs[h, 7, rows(i)] = own(h, 7, i).astype(BF16)
            back(h, 7, i, dev)

    def home(s, _):
        a = 6 - s
        for h, dev in ways:
            wait(cm.at[h, a], cm_recv.at[h, a])
        for i in order:
            for h, dev in ways:
                wait(zr.at[h, a, rows(i)], z_recv.at[h, a, i])
                zs[h, a, rows(i)] = (own(h, a, i) + zr[h, a, rows(i)].astype(F32)).astype(BF16)
                back(h, a, i, dev)
        return 0

    lax.fori_loop(0, 6, home, 0)
    for h, dev in ways:
        wait(cm.at[h, 0], cm_recv.at[h, 0])
    total = None
    for i in order:
        wait(zr.at[1, 0, rows(i)], z_recv.at[1, 0, i])
        zs[1, 0, rows(i)] = (own(1, 0, i) + zr[1, 0, rows(i)].astype(F32)).astype(BF16)
        back(1, 0, i, up_dev)
    for i in order:
        wait(zr.at[0, 0, rows(i)], z_recv.at[0, 0, i])
        wait(zr.at[1, 7, rows(i)], z_recv.at[1, 7, i])
        total = own(0, 0, i) + zr[0, 0, rows(i)].astype(F32) + zr[1, 7, rows(i)].astype(F32)
        if i:
            fs[i - 1] = total.astype(BF16)
            send(fs.at[i - 1], yr.at[i - 1], f_send, f_recv, sub_dev(i))

    ctx_out.wait()
    wait(xb.at[0, 0, 0, 0 : 3 * TOK], y_send)
    wait(xb.at[0, 0:7, 0], ring_send)
    wait(xb.at[1, :, 0], ring_send)
    wait(xb.at[0, :, 0], mate_send)
    wait(xb.at[1, :, 0], mate_send)
    wait(rp, rp_send)
    for u in range(4):
        wait(hr.at[u, 0:7], h_send)
    wait(cs, cm_send)
    wait(zs.at[0, 0:7], z_send)
    wait(zs.at[1], z_send)
    wait(fs, f_send)

    wait(yr, f_recv)
    for n in range(3):
        total = total + yr[n].astype(F32)
    moe_ref[...] = total.astype(BF16)


def per_device(x_a, routes, route_score, w_gate, w_up, w_down, queries, cache, lengths):
    vmem = pl.BlockSpec(memory_space=pltpu.VMEM)
    hbm = pl.BlockSpec(memory_space=pl.ANY)
    dma, dmas = pltpu.SemaphoreType.DMA, lambda *s: pltpu.SemaphoreType.DMA(s)
    return pl.pallas_call(
        kernel,
        out_shape=(
            jax.ShapeDtypeStruct((TOK, WIDTH), BF16),
            jax.ShapeDtypeStruct((1, 128, KV_RANK), BF16),
        ),
        in_specs=[vmem] * 4 + [hbm] * 5,
        out_specs=(vmem, hbm),
        scratch_shapes=[
            pltpu.VMEM((2, 8, 2, 64, WIDE), BF16),
            pltpu.VMEM((WIDTH, FFS), BF16),
            pltpu.VMEM((WIDTH, FFS), BF16),
            pltpu.VMEM((FFS, WIDTH), BF16),
            pltpu.VMEM((128, 576), BF16),
            pltpu.VMEM((128, 576), BF16),
            pltpu.VMEM((128, KV_RANK), BF16),
            pltpu.VMEM((8, 4, GROUP, 2 * SHARE), BF16),
            pltpu.VMEM((4, 7, GROUP, 2 * SHARE), BF16),
            pltpu.VMEM((4, 8, GROUP, SHARE), BF16),
            pltpu.VMEM((2, 8, 64, WIDTH), F32),
            pltpu.VMEM((2, 8, 64, WIDTH), BF16),
            pltpu.VMEM((2, 8, 64, WIDTH), BF16),
            pltpu.VMEM((2, 8, 64, WIDTH), BF16),
            pltpu.VMEM((2, 8, 64, WIDTH), BF16),
            pltpu.VMEM((3, TOK, WIDTH), BF16),
            pltpu.VMEM((3, TOK, WIDTH), BF16),
            dmas(6), dma, dmas(4), dma, dmas(2, 8, 4), dma, dmas(2, 8),
            dma, dmas(4), dma, dmas(4), dma, dmas(2, 8), dma, dmas(2, 8, 4), dma, dma,
        ],
        compiler_params=pltpu.CompilerParams(
            collective_id=0, has_side_effects=True, vmem_limit_bytes=48 << 20
        ),
        name="moe_attention",
    )(x_a, routes, route_score, lengths.reshape(1, 1), w_gate, w_up, w_down, queries, cache)


def solution(mesh):
    placed = (
        P(("peer", "sub"), "pool"),
        P(("peer", "sub"), None),
        P(("peer", "sub"), None),
        P("peer", "pool", "sub"),
        P("peer", "pool", "sub"),
        P("peer", "sub", "pool"),
        P(("pool", "peer", "sub"), None, None),
        P(("pool", "peer", "sub"), None, None),
        P(("pool", "peer", "sub")),
    )
    return jax.shard_map(
        per_device,
        mesh=mesh,
        in_specs=placed,
        out_specs=(P(("peer", "sub"), "pool"), P(("pool", "peer", "sub"), None, None)),
        check_vma=False,
    )
```

time: 428 us -> 111 us (0.26)
  blocking collectives: 197 us -> 0 us
  waiting for transfers between devices: 195 us -> 0 us
  Pallas kernels: 0 us -> 101 us
  between operations: 14.5 us -> 1.32 us
  matrix products: 10.1 us -> 0 us
    all_to_all x2 -> x0, blocking collectives: 197 us -> none  [the longest x1 123 us: per_device(): lax.all_to_all(partial_out, 'peer', split_axis=1, concat_axis=1, tiled=True)]
    pallas_call x0 -> x1, Pallas kernels: none -> 101 us  [per_device(): pl.pallas_call(kernel, out_shape=(jax.ShapeDtypeStruct((TOK, WIDTH), BF16...]
    psum x1 -> x0, waiting for transfers between devices: 93.9 us -> none  [per_device(): gate_full, upper_full = lax.psum((gate_part, upper_part), 'pool')]
    all_gather x1 -> x0, waiting for transfers between devices: 52.1 us -> none  [per_device(): grouped = lax.all_gather(outgoing[None], 'sub', axis=0, tiled=True)]
    reduce_scatter x1 -> x0, waiting for transfers between devices: 49 us -> none  [per_device(): summed = lax.psum_scatter(returned, 'sub', scatter_dimension=0, tiled=True)]
    dot_general x9 -> x0, matrix products: 10.1 us -> none  [the longest x1 2.58 us: per_device(): jnp.einsum('rlmf,lfd->rlmd', hidden, w_down, preferred_element_type=jnp.f...]
    unnamed x13 -> x18, local copies, waits for them, and re-layouts: 2.54 us -> 7.48 us
  transfers between devices with their start and end apart: 3 -> 0, of which waited for: 3 -> 0; matrix products, arithmetic and copies ran while one was open for 0% -> 0% of each run, Pallas kernels for 0% -> 0%
where the time goes in v1:
time: 111 us; the launch traced here: 110 us
  Pallas kernels  101 us (91%)
  local copies, waits for them, and re-layouts  7.48 us (7%)
  between operations  1.32 us (1%)
    pallas_call x1, Pallas kernels, per_device(): pl.pallas_call(kernel, out_shape=(jax.ShapeDtypeStruct((TOK, WIDTH), BF16...  101 us
    unnamed x18, local copies, waits for them, and re-layouts  7.48 us

profile of v1, /device:TPU:6, one launch (start us, length us, event | category | flops | bytes accessed | tf_op | source)
XLA Modules:
  0.0 109.6 jit_solution(12889023216883034804)
XLA Ops:
  1.3 0.0 copy-start.5
  1.3 0.8 copy.11.routes_ref
  2.1 0.0 copy-done.5
  2.1 0.1 copy.12.score_ref
  2.1 0.0 copy-start.4
  2.1 1.1 %copy.13.q_hbm = bf16[1,128,576]{2,1,0:T(8,128)(2,1)S(1)} copy(bf16[1,128,576]{1,2,0:T(8,128)(2,1)} %param.15) | data formatting | bytes 294912 | tf_op args[6]
  3.2 0.0 copy-done.4
  3.2 0.0 copy-start.3
  3.2 0.2 copy.14.c_hbm
  3.4 0.6 copy-done.3
  4.0 0.0 copy-start
  4.0 1.2 %copy-done = bf16[1,896,512]{2,1,0:T(8,128)(2,1)S(1)} copy-done((bf16[1,896,512]{2,1,0:T(8,128)(2,1)S(1)}, bf16[1,896,512]{2,1,0:T(8,128)(2,1)}, u32[]{:S(2)}) %copy-start) | copy-done | bytes 917528
  5.2 0.0 copy-start.1
  5.2 1.2 %copy-done.1 = bf16[1,896,512]{2,1,0:T(8,128)(2,1)S(1)} copy-done((bf16[1,896,512]{2,1,0:T(8,128)(2,1)S(1)}, bf16[1,896,512]{2,1,0:T(8,128)(2,1)}, u32[]{:S(2)}) %copy-start.1) | copy-done | bytes 917528
  6.3 0.0 copy-start.2
  6.3 1.2 %copy-done.2 = bf16[1,512,896]{2,1,0:T(8,128)(2,1)S(1)} copy-done((bf16[1,512,896]{2,1,0:T(8,128)(2,1)S(1)}, bf16[1,512,896]{2,1,0:T(8,128)(2,1)}, u32[]{:S(2)}) %copy-start.2) | copy-done | bytes 917528
  7.5 100.8 %moe_attention.1 = (bf16[16,896]{1,0:T(8,128)(2,1)S(1)}, bf16[1,128,512]{2,1,0:T(8,128)(2,1)S(1)}) custom-call(bf16[16,896]{1,0:T(8,128)(2,1)S(1)} %copy-done.3, s32[16,8]{1,0:T(8,128)S(1)} %copy.11.routes_ref, f32[16,8]{1,0:T(8,128)S(1)} %copy.12.score_ref, s32[1,1]{1,0:T(1,128)} %bitcast.1.len_ref, bf16[1,896,512]{2,1,0:T(8,128)(2,1)S(1)} %copy-done, ...), custom_call_target="tpu_custom_call" | custom-call | tf_op jit(solution)/shard_map/moe_attention/pallas_call | solution.py:295
  108.3 0.6 copy.18
  108.9 0.7 copy.19
Async XLA Ops:
  1.3 0.8 copy-start.5
  2.1 1.1 %copy-start.4 = (bf16[1,128,576]{1,2,0:T(8,128)(2,1)S(1)}, bf16[1,128,576]{1,2,0:T(8,128)(2,1)}, u32[]{:S(2)}) copy-start(bf16[1,128,576]{1,2,0:T(8,128)(2,1)} %param.16) | copy-start | bytes 442372
  3.2 0.8 copy-start.3
  4.0 1.2 %copy-start = (bf16[1,896,512]{2,1,0:T(8,128)(2,1)S(1)}, bf16[1,896,512]{2,1,0:T(8,128)(2,1)}, u32[]{:S(2)}) copy-start(bf16[1,896,512]{2,1,0:T(8,128)(2,1)} %wg_hbm.1) | copy-start | bytes 2752516
  5.2 1.2 %copy-start.1 = (bf16[1,896,512]{2,1,0:T(8,128)(2,1)S(1)}, bf16[1,896,512]{2,1,0:T(8,128)(2,1)}, u32[]{:S(2)}) copy-start(bf16[1,896,512]{2,1,0:T(8,128)(2,1)} %wu_hbm.1) | copy-start | bytes 2752516
  6.3 1.2 %copy-start.2 = (bf16[1,512,896]{2,1,0:T(8,128)(2,1)S(1)}, bf16[1,512,896]{2,1,0:T(8,128)(2,1)}, u32[]{:S(2)}) copy-start(bf16[1,512,896]{2,1,0:T(8,128)(2,1)} %wd_hbm.1) | copy-start | bytes 2752516

commit v2 on v1

v2 whole, which is shorter than its diff:
```python
import functools

import jax
import jax.numpy as jnp
from jax import lax
from jax.experimental import pallas as pl
from jax.experimental.pallas import tpu as pltpu
from jax.sharding import PartitionSpec as P

KV_RANK = 512
SCALE = 192 ** (-0.5)
ROUTED = 2.5
TOK = 16
MOST = 5
WIDTH = 896
WIDE = 1024
FFS = 512
HALF = 8 * MOST
GROUP = 2 * HALF
PAD = 48
SHARE = FFS // 4
MESH = pl.DeviceIdType.MESH
F32, BF16 = jnp.float32, jnp.bfloat16


def kernel(
    x_ref, routes_ref, score_ref, len_ref, wg_hbm, wu_hbm, wd_hbm, q_hbm, c_hbm,
    moe_ref, ctx_hbm,
    xb, wg, wu, wd, qv, cv, ctxv, po, pm, pr, sp, rp, hr, yo, ym, ye, co, zs, zr, fs, yr,
    load_sem, y_send, y_recv, ring_send, ring_recv, mate_send, mate_recv,
    rp_send, rp_recv, h_send, h_recv, ym_send, ym_recv, z_send, z_recv, f_send, f_recv,
):
    pool, peer, sub = lax.axis_index("pool"), lax.axis_index("peer"), lax.axis_index("sub")
    row, col = pool // 4, lax.rem(pool, 4)
    up_dev = {"peer": lax.rem(peer + 2, 32)}
    down_dev = {"peer": lax.rem(peer + 30, 32)}
    mate_dev = {"peer": peer + 1 - 2 * lax.rem(peer, 2)}

    def sub_dev(d):
        return {"sub": lax.rem(sub + d, 4)}

    def pool_dev(d):
        return {"pool": lax.rem(pool + d, 8)}

    def send(src, dst, ssem, rsem, dev):
        pltpu.make_async_remote_copy(
            src_ref=src, dst_ref=dst, send_sem=ssem, recv_sem=rsem,
            device_id=dev, device_id_type=MESH,
        ).start()

    def wait(ref, sem):
        pltpu.make_async_copy(ref, ref, sem).wait()

    barrier = pltpu.get_barrier_semaphore()
    partners = [up_dev, down_dev, mate_dev]
    partners += [sub_dev(d) for d in range(1, 4)] + [pool_dev(d) for d in range(1, 8)]
    for dev in partners:
        pl.semaphore_signal(barrier, inc=1, device_id=dev, device_id_type=MESH)

    loads = [
        pltpu.make_async_copy(src, dst, load_sem.at[n])
        for n, (src, dst) in enumerate(
            ((q_hbm.at[0], qv), (c_hbm.at[0], cv), (wg_hbm.at[0], wg), (wu_hbm.at[0], wu), (wd_hbm.at[0], wd))
        )
    ]
    for load in loads:
        load.start()

    lane = lax.broadcasted_iota(jnp.int32, (TOK, 128), 1)
    score = score_ref[...]
    weight = ROUTED * score / jnp.sum(score, axis=0, keepdims=True)
    high = weight.astype(BF16)
    eye = lax.broadcasted_iota(jnp.int32, (8, 8), 0) == lax.broadcasted_iota(jnp.int32, (8, 8), 1)
    eye = jnp.where(eye, 1.0, 0.0).astype(BF16)

    def turn(v):
        return lax.dot_general(v, eye, (((0,), (0,)), ((), ())), preferred_element_type=F32)

    names = turn(routes_ref[...].astype(F32).astype(BF16)).astype(jnp.int32)
    low = turn((weight - high.astype(F32)).astype(BF16))
    high = turn(high)
    hit = jnp.zeros((TOK, 128), F32)
    mix = jnp.zeros((TOK, 128), F32)
    for k in range(8):
        expert = names[:, k : k + 1]
        hit = hit + jnp.where(lane == expert, 1.0, 0.0)
        mix = mix + jnp.where(lane == expert + 32, high[:, k : k + 1], 0.0)
        mix = mix + jnp.where(lane == expert + 64, low[:, k : k + 1], 0.0)
    before = (
        lax.broadcasted_iota(jnp.int32, (TOK, TOK), 1) < lax.broadcasted_iota(jnp.int32, (TOK, TOK), 0)
    )
    earlier = jnp.dot(jnp.where(before, 1.0, 0.0).astype(BF16), hit.astype(BF16), preferred_element_type=F32)
    table = (earlier + 1.0) * hit + mix
    xb[0, 0, 0:TOK, 0:WIDTH] = x_ref[...]
    xb[0, 0, 0:TOK, WIDTH:WIDE] = table.astype(BF16)

    pl.semaphore_wait(barrier, len(partners))

    def rows(i):
        return pl.ds(TOK * i, TOK)

    def pass_up(a, i):
        send(xb.at[0, a, rows(i)], xb.at[0, a + 1, rows(i)], ring_send, ring_recv.at[0, a + 1, i], up_dev)

    def pass_down(a, i):
        send(xb.at[1, a, rows(i)], xb.at[1, a + 1, rows(i)], ring_send, ring_recv.at[1, a + 1, i], down_dev)

    for d in (2, 1, 3):
        send(xb.at[0, 0, rows(0)], xb.at[0, 0, rows(4 - d)], y_send, y_recv.at[4 - d], sub_dev(d))
    for i in (0, 1, 3, 2):
        if i:
            wait(xb.at[0, 0, rows(i)], y_recv.at[i])
        pass_up(0, i)
        send(xb.at[0, 0, rows(i)], xb.at[1, 0, rows(i)], ring_send, ring_recv.at[1, 0, i], down_dev)

    ctx_out = pltpu.make_async_copy(ctxv, ctx_hbm.at[0], load_sem.at[5])

    def attention():
        loads[0].wait()
        loads[1].wait()
        entries = cv[...]
        scores = lax.dot_general(qv[...], entries, (((0,), (0,)), ((), ())), preferred_element_type=F32) * SCALE
        valid = lax.broadcasted_iota(jnp.int32, scores.shape, 1) < len_ref[...]
        top = jnp.max(jnp.where(valid, scores, -jnp.inf), axis=1, keepdims=True)
        expo = jnp.where(valid, jnp.exp(scores - top), 0.0)
        probs = (expo / jnp.sum(expo, axis=1, keepdims=True)).astype(BF16)
        ctxv[...] = lax.dot_general(
            probs, entries[0:KV_RANK], (((1,), (1,)), ((), ())), preferred_element_type=F32
        ).astype(BF16)
        ctx_out.start()

    for load in loads[2:]:
        load.wait()

    def placing(k, expert, first):
        u, h = k // 2, lax.rem(k, 2)
        tab = xb[h, pl.ds(2 * u, 2), :, WIDTH:WIDE].reshape(128, 128).astype(F32)
        lanes = lax.broadcasted_iota(jnp.int32, (128, 128), 1)
        slot = jnp.sum(jnp.where(lanes == expert, tab, 0.0), axis=1, keepdims=True)
        share = jnp.where((lanes == expert + 32) | (lanes == expert + 64), tab, 0.0)
        base = lax.broadcasted_iota(jnp.int32, (128, 1), 0) // TOK * MOST - 1 + first
        place = jnp.where(slot > 0.5, slot.astype(jnp.int32) + base, -1)
        return place, jnp.sum(share, axis=1, keepdims=True)

    mate = peer + 1 - 2 * lax.rem(peer, 2)

    def select(k):
        u, h = k // 2, lax.rem(k, 2)
        mine, _ = placing(k, peer, 0)
        other, _ = placing(k, mate, PAD)
        slots = lax.broadcasted_iota(jnp.int32, (128, 128), 1)
        onehot = jnp.where((slots == mine) | (slots == other), 1.0, 0.0).astype(BF16)
        x = xb[h, pl.ds(2 * u, 2), :, 0:WIDTH].reshape(128, WIDTH)
        picked = lax.dot_general(onehot, x, (((0,), (0,)), ((), ())), preferred_element_type=F32).astype(BF16)
        pm[k] = picked[PAD : 2 * PAD]
        send(pm.at[k], pr.at[k], mate_send, mate_recv.at[k], mate_dev)
        po[k] = picked[0:PAD]

    def gates(k):
        u, h = k // 2, lax.rem(k, 2)
        wait(pr.at[k], mate_recv.at[k])
        picked = jnp.concatenate([po[k].astype(F32)[0:HALF], pr[k].astype(F32)[0:HALF]], axis=0).astype(BF16)
        gate = jnp.dot(picked, wg[...], preferred_element_type=F32).astype(BF16)
        for n in range(4):
            sp[k, n, :, 0:SHARE] = gate[:, SHARE * n : SHARE * (n + 1)]
        upper = jnp.dot(picked, wu[...], preferred_element_type=F32).astype(BF16)
        for n in range(4):
            sp[k, n, :, SHARE : 2 * SHARE] = upper[:, SHARE * n : SHARE * (n + 1)]

        def give(d):
            c = lax.rem(col + d, 4)
            dest = h * 4 + c
            place = lax.rem(pool - dest + 8, 8) - 1
            send(sp.at[k, c], rp.at[u, place], rp_send, rp_recv.at[u], {"pool": dest})

        for d in (2, 1, 3):
            give(d)

        @pl.when(h != row)
        def _():
            give(0)

    def hidden(u):
        wait(rp.at[u], rp_recv.at[u])
        total = sp[2 * u + row, col].astype(F32)
        for n in range(7):
            total = total + rp[u, n].astype(F32)
        gate, upper = total[:, 0:SHARE], total[:, SHARE : 2 * SHARE]
        hr[u, pool] = (gate / (1.0 + jnp.exp(-gate)) * upper).astype(BF16)
        for d in (6, 2, 5, 7, 3, 1, 4):
            send(hr.at[u, pool], hr.at[u, pool], h_send, h_recv.at[u], pool_dev(d))

    def down(u):
        wait(hr.at[u, 0:7], h_recv.at[u])
        for h in range(2):
            k = 2 * u + h
            hid = jnp.concatenate([hr[u, 4 * h + n] for n in range(4)], axis=1)
            out = jnp.dot(hid, wd[...], preferred_element_type=F32)
            none = jnp.zeros((PAD - HALF, WIDTH), F32)
            ym[k] = jnp.concatenate([out[HALF:GROUP], none], axis=0).astype(BF16)
            send(ym.at[k], ye.at[k], ym_send, ym_recv.at[k], mate_dev)
            yo[k] = jnp.concatenate([out[0:HALF], none], axis=0).astype(BF16)

    def combine(k):
        u, h = k // 2, lax.rem(k, 2)
        wait(ye.at[k], ym_recv.at[k])
        slots = lax.broadcasted_iota(jnp.int32, (128, PAD), 1)
        total = None
        for expert, part in ((peer, yo), (mate, ye)):
            place, wt = placing(k, expert, 0)
            onehot = jnp.where(slots == place, 1.0, 0.0).astype(BF16)
            term = wt * jnp.dot(onehot, part[k], preferred_element_type=F32)
            total = term if total is None else total + term
        co[h, pl.ds(2 * u, 2)] = total.reshape(2, 64, WIDTH)

    def hop(t, _):
        @pl.when(t <= 8)
        def _():
            for i in (0, 1, 3, 2):
                @pl.when(t <= 7)
                def _():
                    wait(xb.at[0, t, rows(i)], ring_recv.at[0, t, i])

                @pl.when(t <= 6)
                def _():
                    pass_up(t, i)

                wait(xb.at[1, t - 1, rows(i)], ring_recv.at[1, t - 1, i])

                @pl.when(t <= 7)
                def _():
                    pass_down(t - 1, i)

            select(t - 1)

        @pl.when(t >= 2)
        def _():
            gates(t - 2)

        @pl.when((t >= 5) & (lax.rem(t, 2) == 1))
        def _():
            hidden((t - 5) // 2)

        @pl.when((t >= 7) & (lax.rem(t, 2) == 1))
        def _():
            down((t - 7) // 2)

        return 0

    lax.fori_loop(1, 10, hop, 0)
    attention()
    hidden(3)
    down(2)

    def mixes(k, _):
        combine(k)
        return 0

    lax.fori_loop(0, 4, mixes, 0)
    down(3)
    lax.fori_loop(4, 8, mixes, 0)

    def own(h, a, i):
        return co[h, a, rows(i)]

    def back(h, a, i, dev):
        after = lax.rem(a + 7, 8)
        send(zs.at[h, a, rows(i)], zr.at[h, after, rows(i)], z_send, z_recv.at[h, after, i], dev)

    ways = ((0, down_dev), (1, up_dev))
    order = (2, 1, 3, 0)
    for i in order:
        for h, dev in ways:
            zs[h, 7, rows(i)] = own(h, 7, i).astype(BF16)
            back(h, 7, i, dev)

    def home(s, _):
        a = 6 - s
        for i in order:
            for h, dev in ways:
                wait(zr.at[h, a, rows(i)], z_recv.at[h, a, i])
                zs[h, a, rows(i)] = (own(h, a, i) + zr[h, a, rows(i)].astype(F32)).astype(BF16)
                back(h, a, i, dev)
        return 0

    lax.fori_loop(0, 6, home, 0)
    total = None
    for i in order:
        wait(zr.at[1, 0, rows(i)], z_recv.at[1, 0, i])
        zs[1, 0, rows(i)] = (own(1, 0, i) + zr[1, 0, rows(i)].astype(F32)).astype(BF16)
        back(1, 0, i, up_dev)
    for i in order:
        wait(zr.at[0, 0, rows(i)], z_recv.at[0, 0, i])
        wait(zr.at[1, 7, rows(i)], z_recv.at[1, 7, i])
        total = own(0, 0, i) + zr[0, 0, rows(i)].astype(F32) + zr[1, 7, rows(i)].astype(F32)
        if i:
            fs[i - 1] = total.astype(BF16)
            send(fs.at[i - 1], yr.at[i - 1], f_send, f_recv, sub_dev(i))

    ctx_out.wait()
    wait(xb.at[0, 0, 0 : 3 * TOK], y_send)
    wait(xb.at[0, 0:7], ring_send)
    wait(xb.at[1], ring_send)
    wait(pm, mate_send)
    wait(rp, rp_send)
    for u in range(4):
        wait(hr.at[u, 0:7], h_send)
    wait(ym, ym_send)
    wait(zs.at[0, 0:7], z_send)
    wait(zs.at[1], z_send)
    wait(fs, f_send)

    wait(yr, f_recv)
    for n in range(3):
        total = total + yr[n].astype(F32)
    moe_ref[...] = total.astype(BF16)


def per_device(x_a, routes, route_score, w_gate, w_up, w_down, queries, cache, lengths):
    vmem = pl.BlockSpec(memory_space=pltpu.VMEM)
    hbm = pl.BlockSpec(memory_space=pltpu.HBM)
    dma, dmas = pltpu.SemaphoreType.DMA, lambda *s: pltpu.SemaphoreType.DMA(s)
    return pl.pallas_call(
        kernel,
        out_shape=(
            jax.ShapeDtypeStruct((TOK, WIDTH), BF16),
            jax.ShapeDtypeStruct((1, 128, KV_RANK), BF16),
        ),
        in_specs=[vmem] * 4 + [hbm] * 5,
        out_specs=(vmem, hbm),
        scratch_shapes=[
            pltpu.VMEM((2, 8, 64, WIDE), BF16),
            pltpu.VMEM((WIDTH, FFS), BF16),
            pltpu.VMEM((WIDTH, FFS), BF16),
            pltpu.VMEM((FFS, WIDTH), BF16),
            pltpu.VMEM((576, 128), BF16),
            pltpu.VMEM((576, 128), BF16),
            pltpu.VMEM((128, KV_RANK), BF16),
            pltpu.VMEM((8, PAD, WIDTH), BF16),
            pltpu.VMEM((8, PAD, WIDTH), BF16),
            pltpu.VMEM((8, PAD, WIDTH), BF16),
            pltpu.VMEM((8, 4, GROUP, 2 * SHARE), BF16),
            pltpu.VMEM((4, 7, GROUP, 2 * SHARE), BF16),
            pltpu.VMEM((4, 8, GROUP, SHARE), BF16),
            pltpu.VMEM((8, PAD, WIDTH), BF16),
            pltpu.VMEM((8, PAD, WIDTH), BF16),
            pltpu.VMEM((8, PAD, WIDTH), BF16),
            pltpu.VMEM((2, 8, 64, WIDTH), F32),
            pltpu.VMEM((2, 8, 64, WIDTH), BF16),
            pltpu.VMEM((2, 8, 64, WIDTH), BF16),
            pltpu.VMEM((3, TOK, WIDTH), BF16),
            pltpu.VMEM((3, TOK, WIDTH), BF16),
            dmas(6), dma, dmas(4), dma, dmas(2, 8, 4), dma, dmas(8),
            dma, dmas(4), dma, dmas(4), dma, dmas(8), dma, dmas(2, 8, 4), dma, dma,
        ],
        compiler_params=pltpu.CompilerParams(
            collective_id=0, has_side_effects=True, vmem_limit_bytes=255 << 18
        ),
        name="moe_attention",
    )(
        x_a, routes.T, route_score.T, lengths.reshape(1, 1), w_gate, w_up, w_down,
        jnp.swapaxes(queries, 1, 2), jnp.swapaxes(cache, 1, 2),
    )


def solution(mesh):
    placed = (
        P(("peer", "sub"), "pool"),
        P(("peer", "sub"), None),
        P(("peer", "sub"), None),
        P("peer", "pool", "sub"),
        P("peer", "pool", "sub"),
        P("peer", "sub", "pool"),
        P(("pool", "peer", "sub"), None, None),
        P(("pool", "peer", "sub"), None, None),
        P(("pool", "peer", "sub")),
    )
    return jax.shard_map(
        per_device,
        mesh=mesh,
        in_specs=placed,
        out_specs=(P(("peer", "sub"), "pool"), P(("pool", "peer", "sub"), None, None)),
        check_vma=False,
    )
```

time: 111 us -> 108 us (0.973)
  local copies, waits for them, and re-layouts: 7.48 us -> 2.93 us
  Pallas kernels: 101 us -> 103 us
    unnamed x18 -> x2, local copies, waits for them, and re-layouts: 7.48 us -> 2.93 us
    pallas_call x1, Pallas kernels: 101 us -> 103 us  [per_device(): pl.pallas_call(kernel, out_shape=(jax.ShapeDtypeStruct((TOK, WIDTH), BF16...]
where the time goes in v2:
time: 108 us; the launch traced here: 107 us
  Pallas kernels  103 us (95%)
  local copies, waits for them, and re-layouts  2.93 us (3%)
  between operations  1.29 us (1%)
    pallas_call x1, Pallas kernels, per_device(): pl.pallas_call(kernel, out_shape=(jax.ShapeDtypeStruct((TOK, WIDTH), BF16...  103 us
    unnamed x2, local copies, waits for them, and re-layouts  2.93 us

profile of v2, /device:TPU:6, one launch (start us, length us, event | category | flops | bytes accessed | tf_op | source)
XLA Modules:
  0.0 107.4 jit_solution(7424085104257891463)
XLA Ops:
  1.3 103.2 %moe_attention.1 = (bf16[16,896]{1,0:T(8,128)(2,1)}, bf16[1,128,512]{2,1,0:T(8,128)(2,1)}) custom-call(bf16[16,896]{1,0:T(8,128)(2,1)} %x_ref.1, s32[8,16]{1,0:T(8,128)} %bitcast.8, f32[8,16]{1,0:T(8,128)} %bitcast.9, s32[1,1]{1,0:T(1,128)} %bitcast.5.len_ref, bf16[1,896,512]{2,1,0:T(8,128)(2,1)} %wg_hbm.1, bf16[1,896,512]{2,1,0:T(8,128)(2,1)} %wu_hbm.1, ...), custom_call_target="tpu_custom_call" | custom-call | tf_op jit(solution)/shard_map/moe_attention/pallas_call | solution.py:323
  104.5 1.4 %copy.14 = bf16[16,896]{1,0:T(8,128)(2,1)} copy(bf16[16,896]{1,0:T(8,128)(2,1)} %get-tuple-element.4) | data formatting | bytes 57344
  105.8 1.6 %copy.15 = bf16[1,128,512]{2,1,0:T(8,128)(2,1)} copy(bf16[1,128,512]{2,1,0:T(8,128)(2,1)} %get-tuple-element.5) | data formatting | bytes 262144

commit v3 on v2

--- a/solution.py
+++ b/solution.py
@@ -26,7 +26,7 @@
 def kernel(
     x_ref, routes_ref, score_ref, len_ref, wg_hbm, wu_hbm, wd_hbm, q_hbm, c_hbm,
     moe_ref, ctx_hbm,
-    xb, wg, wu, wd, qv, cv, ctxv, po, pm, pr, sp, rp, hr, yo, ym, ye, co, zs, zr, fs, yr,
+    xb, wg, wu, wd, qv, cv, ctxv, po, pm, pr, pk, sp, rp, hr, yo, ym, ye, co, zs, zr, fs, yr,
     load_sem, y_send, y_recv, ring_send, ring_recv, mate_send, mate_recv,
     rp_send, rp_recv, h_send, h_recv, ym_send, ym_recv, z_send, z_recv, f_send, f_recv,
 ):
@@ -157,13 +157,15 @@
         po[k] = picked[0:PAD]
 
     def gates(k):
-        u, h = k // 2, lax.rem(k, 2)
         wait(pr.at[k], mate_recv.at[k])
-        picked = jnp.concatenate([po[k].astype(F32)[0:HALF], pr[k].astype(F32)[0:HALF]], axis=0).astype(BF16)
-        gate = jnp.dot(picked, wg[...], preferred_element_type=F32).astype(BF16)
+        pk[...] = jnp.concatenate([po[k].astype(F32)[0:HALF], pr[k].astype(F32)[0:HALF]], axis=0).astype(BF16)
+        gate = jnp.dot(pk[...], wg[...], preferred_element_type=F32).astype(BF16)
         for n in range(4):
             sp[k, n, :, 0:SHARE] = gate[:, SHARE * n : SHARE * (n + 1)]
-        upper = jnp.dot(picked, wu[...], preferred_element_type=F32).astype(BF16)
+
+    def uppers(k):
+        u, h = k // 2, lax.rem(k, 2)
+        upper = jnp.dot(pk[...], wu[...], preferred_element_type=F32).astype(BF16)
         for n in range(4):
             sp[k, n, :, SHARE : 2 * SHARE] = upper[:, SHARE * n : SHARE * (n + 1)]
 
@@ -213,86 +215,116 @@
             total = term if total is None else total + term
         co[h, pl.ds(2 * u, 2)] = total.reshape(2, 64, WIDTH)
 
+    above, below = (2, 1), (3, 0)
+
     def hop(t, _):
-        @pl.when(t <= 8)
-        def _():
-            for i in (0, 1, 3, 2):
-                @pl.when(t <= 7)
+        for n, i in enumerate((0, 1, 3, 2)):
+            @pl.when(t <= 7)
+            def _():
+                wait(xb.at[0, t, rows(i)], ring_recv.at[0, t, i])
+
+            @pl.when(t <= (7 if i in above else 6))
+            def _():
+                way, place = t // 7, jnp.minimum(t + 1, 7)
+                send(xb.at[0, t, rows(i)], xb.at[way, place, rows(i)], ring_send, ring_recv.at[way, place, i], up_dev)
+
+            wait(xb.at[1, t - 1, rows(i)], ring_recv.at[1, t - 1, i])
+
+            @pl.when(t <= (6 if i in above else 7))
+            def _():
+                pass_down(t - 1, i)
+
+            if n == 0:
+                @pl.when(t >= 3)
                 def _():
-                    wait(xb.at[0, t, rows(i)], ring_recv.at[0, t, i])
-
-                @pl.when(t <= 6)
+                    gates(t - 3)
+            elif n == 1:
+                @pl.when(t >= 3)
                 def _():
-                    pass_up(t, i)
-
-                wait(xb.at[1, t - 1, rows(i)], ring_recv.at[1, t - 1, i])
-
-                @pl.when(t <= 7)
+                    uppers(t - 3)
+            elif n == 2:
+                @pl.when((t == 6) | (t == 8))
                 def _():
-                    pass_down(t - 1, i)
-
-            select(t - 1)
-
-        @pl.when(t >= 2)
-        def _():
-            gates(t - 2)
-
-        @pl.when((t >= 5) & (lax.rem(t, 2) == 1))
-        def _():
-            hidden((t - 5) // 2)
-
-        @pl.when((t >= 7) & (lax.rem(t, 2) == 1))
-        def _():
-            down((t - 7) // 2)
+                    hidden((t - 6) // 2)
+            else:
+                @pl.when(t >= 2)
+                def _():
+                    select(t - 2)
 
         return 0
 
-    lax.fori_loop(1, 10, hop, 0)
-    attention()
-    hidden(3)
-    down(2)
+    lax.fori_loop(1, 9, hop, 0)
+    select(7)
+
+    def last(k, _):
+        gates(k)
+        uppers(k)
+        return 0
+
+    lax.fori_loop(6, 8, last, 0)
 
     def mixes(k, _):
         combine(k)
         return 0
 
+    def downs(u, _):
+        down(u)
+        return 0
+
+    attention()
+    hidden(2)
+    lax.fori_loop(0, 2, downs, 0)
+    hidden(3)
+    down(2)
     lax.fori_loop(0, 4, mixes, 0)
     down(3)
     lax.fori_loop(4, 8, mixes, 0)
 
-    def own(h, a, i):
-        return co[h, a, rows(i)]
-
-    def back(h, a, i, dev):
-        after = lax.rem(a + 7, 8)
-        send(zs.at[h, a, rows(i)], zr.at[h, after, rows(i)], z_send, z_recv.at[h, after, i], dev)
-
-    ways = ((0, down_dev), (1, up_dev))
-    order = (2, 1, 3, 0)
+    def back(h, a, i, way, place):
+        send(
+            zs.at[h, a, rows(i)], zr.at[way, place, rows(i)], z_send, z_recv.at[way, place, i],
+            down_dev if way == 0 else up_dev,
+        )
+
+    def start(h, a, i, way, place):
+        zs[h, a, rows(i)] = co[h, a, rows(i)].astype(BF16)
+        back(h, a, i, way, place)
+
+    def onward(h, a, i):
+        wait(zr.at[h, a, rows(i)], z_recv.at[h, a, i])
+        zs[h, a, rows(i)] = (co[h, a, rows(i)] + zr[h, a, rows(i)].astype(F32)).astype(BF16)
+        back(h, a, i, h, lax.rem(a + 7, 8))
+
+    order = (2, 3, 1, 0)
     for i in order:
-        for h, dev in ways:
-            zs[h, 7, rows(i)] = own(h, 7, i).astype(BF16)
-            back(h, 7, i, dev)
+        if i in above:
+            start(1, 7, i, 0, 7)
+            start(1, 6, i, 1, 5)
+        else:
+            start(0, 7, i, 0, 6)
+            start(1, 7, i, 1, 6)
 
     def home(s, _):
-        a = 6 - s
         for i in order:
-            for h, dev in ways:
-                wait(zr.at[h, a, rows(i)], z_recv.at[h, a, i])
-                zs[h, a, rows(i)] = (own(h, a, i) + zr[h, a, rows(i)].astype(F32)).astype(BF16)
-                back(h, a, i, dev)
+            if i in above:
+                onward(0, 8 - s, i)
+                onward(1, 6 - s, i)
+            else:
+                onward(0, 7 - s, i)
+                onward(1, 7 - s, i)
         return 0
 
-    lax.fori_loop(0, 6, home, 0)
+    lax.fori_loop(1, 7, home, 0)
+    for i in order:
+        if i in above:
+            onward(0, 1, i)
+        else:
+            onward(1, 0, i)
     total = None
-    for i in order:
-        wait(zr.at[1, 0, rows(i)], z_recv.at[1, 0, i])
-        zs[1, 0, rows(i)] = (own(1, 0, i) + zr[1, 0, rows(i)].astype(F32)).astype(BF16)
-        back(1, 0, i, up_dev)
     for i in order:
         wait(zr.at[0, 0, rows(i)], z_recv.at[0, 0, i])
         wait(zr.at[1, 7, rows(i)], z_recv.at[1, 7, i])
-        total = own(0, 0, i) + zr[0, 0, rows(i)].astype(F32) + zr[1, 7, rows(i)].astype(F32)
+        total = co[0, 0, rows(i)] + zr[0, 0, rows(i)].astype(F32) + zr[1, 7, rows(i)].astype(F32)
         if i:
             fs[i - 1] = total.astype(BF16)
             send(fs.at[i - 1], yr.at[i - 1], f_send, f_recv, sub_dev(i))
@@ -339,6 +371,7 @@
             pltpu.VMEM((8, PAD, WIDTH), BF16),
             pltpu.VMEM((8, PAD, WIDTH), BF16),
             pltpu.VMEM((8, PAD, WIDTH), BF16),
+            pltpu.VMEM((GROUP, WIDTH), BF16),
             pltpu.VMEM((8, 4, GROUP, 2 * SHARE), BF16),
             pltpu.VMEM((4, 7, GROUP, 2 * SHARE), BF16),
             pltpu.VMEM((4, 8, GROUP, SHARE), BF16),

time: 108 us -> 110 us (1.019)
  Pallas kernels: 103 us -> 105 us
    pallas_call x1, Pallas kernels: 103 us -> 105 us  [per_device(): pl.pallas_call(kernel, out_shape=(jax.ShapeDtypeStruct((TOK, WIDTH), BF16...]
where the time goes in v3:
time: 110 us
  Pallas kernels  105 us (95%)
  local copies, waits for them, and re-layouts  2.93 us (3%)
  between operations  1.29 us (1%)
    pallas_call x1, Pallas kernels, per_device(): pl.pallas_call(kernel, out_shape=(jax.ShapeDtypeStruct((TOK, WIDTH), BF16...  105 us
    unnamed x2, local copies, waits for them, and re-layouts  2.93 us

profile of v3, /device:TPU:6, one launch (start us, length us, event | category | flops | bytes accessed | tf_op | source)
XLA Modules:
  0.0 109.5 jit_solution(2954565827662179721)
XLA Ops:
  1.3 105.3 %moe_attention.1 = (bf16[16,896]{1,0:T(8,128)(2,1)}, bf16[1,128,512]{2,1,0:T(8,128)(2,1)}) custom-call(bf16[16,896]{1,0:T(8,128)(2,1)} %x_ref.1, s32[8,16]{1,0:T(8,128)} %bitcast.8, f32[8,16]{1,0:T(8,128)} %bitcast.9, s32[1,1]{1,0:T(1,128)} %bitcast.5.len_ref, bf16[1,896,512]{2,1,0:T(8,128)(2,1)} %wg_hbm.1, bf16[1,896,512]{2,1,0:T(8,128)(2,1)} %wu_hbm.1, ...), custom_call_target="tpu_custom_call" | custom-call | tf_op jit(solution)/shard_map/moe_attention/pallas_call | solution.py:355
  106.6 1.4 %copy.14 = bf16[16,896]{1,0:T(8,128)(2,1)} copy(bf16[16,896]{1,0:T(8,128)(2,1)} %get-tuple-element.4) | data formatting | bytes 57344
  108.0 1.6 %copy.15 = bf16[1,128,512]{2,1,0:T(8,128)(2,1)} copy(bf16[1,128,512]{2,1,0:T(8,128)(2,1)} %get-tuple-element.5) | data formatting | bytes 262144

commit v4 on v2

--- a/solution.py
+++ b/solution.py
@@ -24,9 +24,9 @@
 
 
 def kernel(
-    x_ref, routes_ref, score_ref, len_ref, wg_hbm, wu_hbm, wd_hbm, q_hbm, c_hbm,
+    x_hbm, routes_hbm, score_hbm, len_ref, wg_hbm, wu_hbm, wd_hbm, q_hbm, c_hbm,
     moe_ref, ctx_hbm,
-    xb, wg, wu, wd, qv, cv, ctxv, po, pm, pr, sp, rp, hr, yo, ym, ye, co, zs, zr, fs, yr,
+    routes_ref, score_ref, xb, wg, wu, wd, qv, cv, ctxv, fact, po, pm, pr, sp, rp, hr, yo, ym, ye, co, zs, zr, fs, yr,
     load_sem, y_send, y_recv, ring_send, ring_recv, mate_send, mate_recv,
     rp_send, rp_recv, h_send, h_recv, ym_send, ym_recv, z_send, z_recv, f_send, f_recv,
 ):
@@ -52,19 +52,24 @@
         pltpu.make_async_copy(ref, ref, sem).wait()
 
     barrier = pltpu.get_barrier_semaphore()
-    partners = [up_dev, down_dev, mate_dev]
-    partners += [sub_dev(d) for d in range(1, 4)] + [pool_dev(d) for d in range(1, 8)]
+    partners = [sub_dev(2), sub_dev(1), sub_dev(3), up_dev, down_dev, mate_dev]
+    partners += [pool_dev(d) for d in (6, 2, 5, 7, 3, 1, 4)]
     for dev in partners:
         pl.semaphore_signal(barrier, inc=1, device_id=dev, device_id_type=MESH)
 
     loads = [
         pltpu.make_async_copy(src, dst, load_sem.at[n])
         for n, (src, dst) in enumerate(
-            ((q_hbm.at[0], qv), (c_hbm.at[0], cv), (wg_hbm.at[0], wg), (wu_hbm.at[0], wu), (wd_hbm.at[0], wd))
+            (
+                (routes_hbm, routes_ref), (score_hbm, score_ref), (x_hbm, xb.at[0, 0, 0:TOK, 0:WIDTH]),
+                (wg_hbm.at[0], wg), (wu_hbm.at[0], wu), (q_hbm.at[0], qv), (c_hbm.at[0], cv), (wd_hbm.at[0], wd),
+            )
         )
     ]
     for load in loads:
         load.start()
+    loads[0].wait()
+    loads[1].wait()
 
     lane = lax.broadcasted_iota(jnp.int32, (TOK, 128), 1)
     score = score_ref[...]
@@ -91,9 +96,9 @@
     )
     earlier = jnp.dot(jnp.where(before, 1.0, 0.0).astype(BF16), hit.astype(BF16), preferred_element_type=F32)
     table = (earlier + 1.0) * hit + mix
-    xb[0, 0, 0:TOK, 0:WIDTH] = x_ref[...]
     xb[0, 0, 0:TOK, WIDTH:WIDE] = table.astype(BF16)
 
+    loads[2].wait()
     pl.semaphore_wait(barrier, len(partners))
 
     def rows(i):
@@ -113,14 +118,14 @@
         pass_up(0, i)
         send(xb.at[0, 0, rows(i)], xb.at[1, 0, rows(i)], ring_send, ring_recv.at[1, 0, i], down_dev)
 
-    ctx_out = pltpu.make_async_copy(ctxv, ctx_hbm.at[0], load_sem.at[5])
+    ctx_out = pltpu.make_async_copy(ctxv, ctx_hbm.at[0], load_sem.at[8])
 
     def attention():
-        loads[0].wait()
-        loads[1].wait()
+        loads[5].wait()
+        loads[6].wait()
         entries = cv[...]
         scores = lax.dot_general(qv[...], entries, (((0,), (0,)), ((), ())), preferred_element_type=F32) * SCALE
-        valid = lax.broadcasted_iota(jnp.int32, scores.shape, 1) < len_ref[...]
+        valid = lax.broadcasted_iota(jnp.int32, scores.shape, 1) < len_ref[0]
         top = jnp.max(jnp.where(valid, scores, -jnp.inf), axis=1, keepdims=True)
         expo = jnp.where(valid, jnp.exp(scores - top), 0.0)
         probs = (expo / jnp.sum(expo, axis=1, keepdims=True)).astype(BF16)
@@ -129,25 +134,27 @@
         ).astype(BF16)
         ctx_out.start()
 
-    for load in loads[2:]:
-        load.wait()
-
-    def placing(k, expert, first):
-        u, h = k // 2, lax.rem(k, 2)
-        tab = xb[h, pl.ds(2 * u, 2), :, WIDTH:WIDE].reshape(128, 128).astype(F32)
-        lanes = lax.broadcasted_iota(jnp.int32, (128, 128), 1)
-        slot = jnp.sum(jnp.where(lanes == expert, tab, 0.0), axis=1, keepdims=True)
-        share = jnp.where((lanes == expert + 32) | (lanes == expert + 64), tab, 0.0)
-        base = lax.broadcasted_iota(jnp.int32, (128, 1), 0) // TOK * MOST - 1 + first
-        place = jnp.where(slot > 0.5, slot.astype(jnp.int32) + base, -1)
-        return place, jnp.sum(share, axis=1, keepdims=True)
+    loads[3].wait()
+    loads[4].wait()
+    loads[7].wait()
 
     mate = peer + 1 - 2 * lax.rem(peer, 2)
+    lanes = lax.broadcasted_iota(jnp.int32, (128, 8), 0)
+    wants = lax.broadcasted_iota(jnp.int32, (128, 8), 1)
+    expert = jnp.where(lax.rem(wants, 2) == 0, peer, mate)
+    slot_of = (wants < 2) & (lanes == expert)
+    share_of = (wants >= 2) & (wants < 4) & ((lanes == expert + 32) | (lanes == expert + 64))
+    reader = jnp.where(slot_of | share_of, 1.0, 0.0).astype(BF16)
+    base = lax.broadcasted_iota(jnp.int32, (128, 1), 0) // TOK * MOST - 1
 
     def select(k):
         u, h = k // 2, lax.rem(k, 2)
-        mine, _ = placing(k, peer, 0)
-        other, _ = placing(k, mate, PAD)
+        tab = xb[h, pl.ds(2 * u, 2), :, WIDTH:WIDE].reshape(128, 128)
+        facts = jnp.dot(tab, reader, preferred_element_type=F32)
+        fact[k] = facts
+        slot = facts.astype(jnp.int32)
+        mine = jnp.where(slot[:, 0:1] > 0, slot[:, 0:1] + base, -1)
+        other = jnp.where(slot[:, 1:2] > 0, slot[:, 1:2] + base + PAD, -1)
         slots = lax.broadcasted_iota(jnp.int32, (128, 128), 1)
         onehot = jnp.where((slots == mine) | (slots == other), 1.0, 0.0).astype(BF16)
         x = xb[h, pl.ds(2 * u, 2), :, 0:WIDTH].reshape(128, WIDTH)
@@ -205,11 +212,13 @@
         u, h = k // 2, lax.rem(k, 2)
         wait(ye.at[k], ym_recv.at[k])
         slots = lax.broadcasted_iota(jnp.int32, (128, PAD), 1)
+        facts = fact[k]
+        slot = facts.astype(jnp.int32)
         total = None
-        for expert, part in ((peer, yo), (mate, ye)):
-            place, wt = placing(k, expert, 0)
+        for n, part in enumerate((yo, ye)):
+            place = jnp.where(slot[:, n : n + 1] > 0, slot[:, n : n + 1] + base, -1)
             onehot = jnp.where(slots == place, 1.0, 0.0).astype(BF16)
-            term = wt * jnp.dot(onehot, part[k], preferred_element_type=F32)
+            term = facts[:, n + 2 : n + 3] * jnp.dot(onehot, part[k], preferred_element_type=F32)
             total = term if total is None else total + term
         co[h, pl.ds(2 * u, 2)] = total.reshape(2, 64, WIDTH)
 
@@ -316,6 +325,10 @@
     moe_ref[...] = total.astype(BF16)
 
 
+def keep(v):
+    return pltpu.with_memory_space_constraint(v, pltpu.HBM)
+
+
 def per_device(x_a, routes, route_score, w_gate, w_up, w_down, queries, cache, lengths):
     vmem = pl.BlockSpec(memory_space=pltpu.VMEM)
     hbm = pl.BlockSpec(memory_space=pltpu.HBM)
@@ -326,9 +339,11 @@
             jax.ShapeDtypeStruct((TOK, WIDTH), BF16),
             jax.ShapeDtypeStruct((1, 128, KV_RANK), BF16),
         ),
-        in_specs=[vmem] * 4 + [hbm] * 5,
-        out_specs=(vmem, hbm),
+        in_specs=[hbm] * 3 + [pl.BlockSpec(memory_space=pltpu.SMEM)] + [hbm] * 5,
+        out_specs=(vmem, pl.BlockSpec(memory_space=pl.ANY)),
         scratch_shapes=[
+            pltpu.VMEM((8, TOK), jnp.int32),
+            pltpu.VMEM((8, TOK), F32),
             pltpu.VMEM((2, 8, 64, WIDE), BF16),
             pltpu.VMEM((WIDTH, FFS), BF16),
             pltpu.VMEM((WIDTH, FFS), BF16),
@@ -336,6 +351,7 @@
             pltpu.VMEM((576, 128), BF16),
             pltpu.VMEM((576, 128), BF16),
             pltpu.VMEM((128, KV_RANK), BF16),
+            pltpu.VMEM((8, 128, 8), F32),
             pltpu.VMEM((8, PAD, WIDTH), BF16),
             pltpu.VMEM((8, PAD, WIDTH), BF16),
             pltpu.VMEM((8, PAD, WIDTH), BF16),
@@ -350,16 +366,16 @@
             pltpu.VMEM((2, 8, 64, WIDTH), BF16),
             pltpu.VMEM((3, TOK, WIDTH), BF16),
             pltpu.VMEM((3, TOK, WIDTH), BF16),
-            dmas(6), dma, dmas(4), dma, dmas(2, 8, 4), dma, dmas(8),
+            dmas(9), dma, dmas(4), dma, dmas(2, 8, 4), dma, dmas(8),
             dma, dmas(4), dma, dmas(4), dma, dmas(8), dma, dmas(2, 8, 4), dma, dma,
         ],
         compiler_params=pltpu.CompilerParams(
-            collective_id=0, has_side_effects=True, vmem_limit_bytes=255 << 18
+            collective_id=0, has_side_effects=True, vmem_limit_bytes=48 << 20
         ),
         name="moe_attention",
     )(
-        x_a, routes.T, route_score.T, lengths.reshape(1, 1), w_gate, w_up, w_down,
-        jnp.swapaxes(queries, 1, 2), jnp.swapaxes(cache, 1, 2),
+        keep(x_a), keep(routes.T), keep(route_score.T), lengths, keep(w_gate), keep(w_up), keep(w_down),
+        keep(jnp.swapaxes(queries, 1, 2)), keep(jnp.swapaxes(cache, 1, 2)),
     )
 
 

time: 108 us -> 105 us (0.972)
  local copies, waits for them, and re-layouts: 2.93 us -> 1.27 us
    unnamed x2, local copies, waits for them, and re-layouts: 2.93 us -> 1.27 us
where the time goes in v4:
time: 105 us
  Pallas kernels  102 us (97%)
  between operations  1.29 us (1%)
  local copies, waits for them, and re-layouts  1.27 us (1%)
    pallas_call x1, Pallas kernels, per_device(): pl.pallas_call(kernel, out_shape=(jax.ShapeDtypeStruct((TOK, WIDTH), BF16...  102 us

profile of v4, /device:TPU:6, one launch (start us, length us, event | category | flops | bytes accessed | tf_op | source)
XLA Modules:
  0.0 104.8 jit_solution(8768916655571716333)
XLA Ops:
  1.3 102.2 %moe_attention.1 = (bf16[16,896]{1,0:T(8,128)(2,1)S(1)}, bf16[1,128,512]{2,1,0:T(8,128)(2,1)S(1)}) custom-call(bf16[16,896]{1,0:T(8,128)(2,1)} %x_hbm.1, s32[8,16]{1,0:T(8,128)} %bitcast.6, f32[8,16]{1,0:T(8,128)} %bitcast.7, s32[1]{0:T(128)S(6)} %copy.13.len_ref, bf16[1,896,512]{2,1,0:T(8,128)(2,1)} %wg_hbm.1, bf16[1,896,512]{2,1,0:T(8,128)(2,1)} %wu_hbm.1, ...), custom_call_target="tpu_custom_call" | custom-call | tf_op jit(solution)/shard_map/moe_attention/pallas_call | solution.py:336
  103.5 0.6 copy.14
  104.1 0.7 copy.15

commit v5 on v4

--- a/solution.py
+++ b/solution.py
@@ -51,12 +51,6 @@
     def wait(ref, sem):
         pltpu.make_async_copy(ref, ref, sem).wait()
 
-    barrier = pltpu.get_barrier_semaphore()
-    partners = [sub_dev(2), sub_dev(1), sub_dev(3), up_dev, down_dev, mate_dev]
-    partners += [pool_dev(d) for d in (6, 2, 5, 7, 3, 1, 4)]
-    for dev in partners:
-        pl.semaphore_signal(barrier, inc=1, device_id=dev, device_id_type=MESH)
-
     loads = [
         pltpu.make_async_copy(src, dst, load_sem.at[n])
         for n, (src, dst) in enumerate(
@@ -66,7 +60,16 @@
             )
         )
     ]
-    for load in loads:
+    for load in loads[:3]:
+        load.start()
+
+    barrier = pltpu.get_barrier_semaphore()
+    partners = [sub_dev(2), sub_dev(1), sub_dev(3), up_dev, down_dev, mate_dev]
+    partners += [pool_dev(d) for d in (6, 2, 5, 7, 3, 1, 4)]
+    for dev in partners:
+        pl.semaphore_signal(barrier, inc=1, device_id=dev, device_id_type=MESH)
+
+    for load in loads[3:]:
         load.start()
     loads[0].wait()
     loads[1].wait()
@@ -195,18 +198,25 @@
         gate, upper = total[:, 0:SHARE], total[:, SHARE : 2 * SHARE]
         hr[u, pool] = (gate / (1.0 + jnp.exp(-gate)) * upper).astype(BF16)
         for d in (6, 2, 5, 7, 3, 1, 4):
-            send(hr.at[u, pool], hr.at[u, pool], h_send, h_recv.at[u], pool_dev(d))
-
-    def down(u):
-        wait(hr.at[u, 0:7], h_recv.at[u])
-        for h in range(2):
-            k = 2 * u + h
-            hid = jnp.concatenate([hr[u, 4 * h + n] for n in range(4)], axis=1)
-            out = jnp.dot(hid, wd[...], preferred_element_type=F32)
-            none = jnp.zeros((PAD - HALF, WIDTH), F32)
-            ym[k] = jnp.concatenate([out[HALF:GROUP], none], axis=0).astype(BF16)
-            send(ym.at[k], ye.at[k], ym_send, ym_recv.at[k], mate_dev)
-            yo[k] = jnp.concatenate([out[0:HALF], none], axis=0).astype(BF16)
+            send(hr.at[u, pool], hr.at[u, pool], h_send, h_recv.at[u, row], pool_dev(d))
+
+    def down(k):
+        u, h = k // 2, lax.rem(k, 2)
+
+        @pl.when(row == h)
+        def _():
+            wait(hr.at[u, 0:3], h_recv.at[u, h])
+
+        @pl.when(row != h)
+        def _():
+            wait(hr.at[u, 0:4], h_recv.at[u, h])
+
+        hid = jnp.concatenate([hr[u, 4 * h + n] for n in range(4)], axis=1)
+        out = jnp.dot(hid, wd[...], preferred_element_type=F32)
+        none = jnp.zeros((PAD - HALF, WIDTH), F32)
+        ym[k] = jnp.concatenate([out[HALF:GROUP], none], axis=0).astype(BF16)
+        send(ym.at[k], ye.at[k], ym_send, ym_recv.at[k], mate_dev)
+        yo[k] = jnp.concatenate([out[0:HALF], none], axis=0).astype(BF16)
 
     def combine(k):
         u, h = k // 2, lax.rem(k, 2)
@@ -252,56 +262,73 @@
 
         @pl.when((t >= 7) & (lax.rem(t, 2) == 1))
         def _():
-            down((t - 7) // 2)
+            down(t - 7)
+            down(t - 6)
 
         return 0
 
     lax.fori_loop(1, 10, hop, 0)
     attention()
     hidden(3)
-    down(2)
 
     def mixes(k, _):
         combine(k)
         return 0
 
+    def downs(k, _):
+        down(k)
+        return 0
+
+    lax.fori_loop(4, 6, downs, 0)
     lax.fori_loop(0, 4, mixes, 0)
-    down(3)
-    lax.fori_loop(4, 8, mixes, 0)
-
-    def own(h, a, i):
-        return co[h, a, rows(i)]
-
-    def back(h, a, i, dev):
+    down(6)
+    lax.fori_loop(4, 6, mixes, 0)
+    down(7)
+    lax.fori_loop(6, 8, mixes, 0)
+
+    runs = (pl.ds(0, 512), pl.ds(512, WIDTH - 512))
+
+    def back(h, a, i, f, dev):
         after = lax.rem(a + 7, 8)
-        send(zs.at[h, a, rows(i)], zr.at[h, after, rows(i)], z_send, z_recv.at[h, after, i], dev)
-
-    ways = ((0, down_dev), (1, up_dev))
+        send(
+            zs.at[h, a, rows(i), runs[f]], zr.at[h, after, rows(i), runs[f]],
+            z_send, z_recv.at[h, after, 2 * i + f], dev,
+        )
+
+    def arrive(h, a, i, f):
+        wait(zr.at[h, a, rows(i), runs[f]], z_recv.at[h, a, 2 * i + f])
+
+    def onward(h, a, i, f, dev):
+        arrive(h, a, i, f)
+        mine, theirs = co[h, a, rows(i), runs[f]], zr[h, a, rows(i), runs[f]]
+        zs[h, a, rows(i), runs[f]] = (mine + theirs.astype(F32)).astype(BF16)
+        back(h, a, i, f, dev)
+
+    ways = ((1, up_dev), (0, down_dev))
     order = (2, 1, 3, 0)
     for i in order:
-        for h, dev in ways:
-            zs[h, 7, rows(i)] = own(h, 7, i).astype(BF16)
-            back(h, 7, i, dev)
+        for f in range(2):
+            for h, dev in ways:
+                zs[h, 7, rows(i), runs[f]] = co[h, 7, rows(i), runs[f]].astype(BF16)
+                back(h, 7, i, f, dev)
 
     def home(s, _):
-        a = 6 - s
         for i in order:
-            for h, dev in ways:
-                wait(zr.at[h, a, rows(i)], z_recv.at[h, a, i])
-                zs[h, a, rows(i)] = (own(h, a, i) + zr[h, a, rows(i)].astype(F32)).astype(BF16)
-                back(h, a, i, dev)
+            for f in range(2):
+                for h, dev in ways:
+                    onward(h, 6 - s, i, f, dev)
         return 0
 
     lax.fori_loop(0, 6, home, 0)
     total = None
     for i in order:
-        wait(zr.at[1, 0, rows(i)], z_recv.at[1, 0, i])
-        zs[1, 0, rows(i)] = (own(1, 0, i) + zr[1, 0, rows(i)].astype(F32)).astype(BF16)
-        back(1, 0, i, up_dev)
+        for f in range(2):
+            onward(1, 0, i, f, up_dev)
     for i in order:
-        wait(zr.at[0, 0, rows(i)], z_recv.at[0, 0, i])
-        wait(zr.at[1, 7, rows(i)], z_recv.at[1, 7, i])
-        total = own(0, 0, i) + zr[0, 0, rows(i)].astype(F32) + zr[1, 7, rows(i)].astype(F32)
+        for f in range(2):
+            arrive(0, 0, i, f)
+            arrive(1, 7, i, f)
+        total = co[0, 0, rows(i)] + zr[0, 0, rows(i)].astype(F32) + zr[1, 7, rows(i)].astype(F32)
         if i:
             fs[i - 1] = total.astype(BF16)
             send(fs.at[i - 1], yr.at[i - 1], f_send, f_recv, sub_dev(i))
@@ -367,7 +394,7 @@
             pltpu.VMEM((3, TOK, WIDTH), BF16),
             pltpu.VMEM((3, TOK, WIDTH), BF16),
             dmas(9), dma, dmas(4), dma, dmas(2, 8, 4), dma, dmas(8),
-            dma, dmas(4), dma, dmas(4), dma, dmas(8), dma, dmas(2, 8, 4), dma, dma,
+            dma, dmas(4), dma, dmas(4, 2), dma, dmas(8), dma, dmas(2, 8, 8), dma, dma,
         ],
         compiler_params=pltpu.CompilerParams(
             collective_id=0, has_side_effects=True, vmem_limit_bytes=48 << 20

time: 105 us -> 104 us (level)
    pallas_call x1, Pallas kernels: 102 us -> 101 us  [per_device(): pl.pallas_call(kernel, out_shape=(jax.ShapeDtypeStruct((TOK, WIDTH), BF16...]
where the time goes in v5:
time: 104 us; the launch traced here: 103 us
  Pallas kernels  101 us (97%)
  between operations  1.29 us (1%)
  local copies, waits for them, and re-layouts  1.27 us (1%)
    pallas_call x1, Pallas kernels, per_device(): pl.pallas_call(kernel, out_shape=(jax.ShapeDtypeStruct((TOK, WIDTH), BF16...  101 us

profile of v5, /device:TPU:6, one launch (start us, length us, event | category | flops | bytes accessed | tf_op | source)
XLA Modules:
  0.0 103.5 jit_solution(708745193890617644)
XLA Ops:
  1.3 100.9 %moe_attention.1 = (bf16[16,896]{1,0:T(8,128)(2,1)S(1)}, bf16[1,128,512]{2,1,0:T(8,128)(2,1)S(1)}) custom-call(bf16[16,896]{1,0:T(8,128)(2,1)} %x_hbm.1, s32[8,16]{1,0:T(8,128)} %bitcast.6, f32[8,16]{1,0:T(8,128)} %bitcast.7, s32[1]{0:T(128)S(6)} %copy.13.len_ref, bf16[1,896,512]{2,1,0:T(8,128)(2,1)} %wg_hbm.1, bf16[1,896,512]{2,1,0:T(8,128)(2,1)} %wu_hbm.1, ...), custom_call_target="tpu_custom_call" | custom-call | tf_op jit(solution)/shard_map/moe_attention/pallas_call | solution.py:363
  102.2 0.6 copy.14
  102.8 0.7 copy.15

commit v6 on v5

--- a/solution.py
+++ b/solution.py
@@ -151,7 +151,7 @@
     base = lax.broadcasted_iota(jnp.int32, (128, 1), 0) // TOK * MOST - 1
 
     def select(k):
-        u, h = k // 2, lax.rem(k, 2)
+        u, h = k // 2, k - k // 2 * 2
         tab = xb[h, pl.ds(2 * u, 2), :, WIDTH:WIDE].reshape(128, 128)
         facts = jnp.dot(tab, reader, preferred_element_type=F32)
         fact[k] = facts
@@ -167,7 +167,7 @@
         po[k] = picked[0:PAD]
 
     def gates(k):
-        u, h = k // 2, lax.rem(k, 2)
+        u, h = k // 2, k - k // 2 * 2
         wait(pr.at[k], mate_recv.at[k])
         picked = jnp.concatenate([po[k].astype(F32)[0:HALF], pr[k].astype(F32)[0:HALF]], axis=0).astype(BF16)
         gate = jnp.dot(picked, wg[...], preferred_element_type=F32).astype(BF16)
@@ -186,7 +186,7 @@
         for d in (2, 1, 3):
             give(d)
 
-        @pl.when(h != row)
+        @pl.when(row != h)
         def _():
             give(0)
 
@@ -201,7 +201,7 @@
             send(hr.at[u, pool], hr.at[u, pool], h_send, h_recv.at[u, row], pool_dev(d))
 
     def down(k):
-        u, h = k // 2, lax.rem(k, 2)
+        u, h = k // 2, k - k // 2 * 2
 
         @pl.when(row == h)
         def _():
@@ -219,7 +219,7 @@
         yo[k] = jnp.concatenate([out[0:HALF], none], axis=0).astype(BF16)
 
     def combine(k):
-        u, h = k // 2, lax.rem(k, 2)
+        u, h = k // 2, k - k // 2 * 2
         wait(ye.at[k], ym_recv.at[k])
         slots = lax.broadcasted_iota(jnp.int32, (128, PAD), 1)
         facts = fact[k]
@@ -233,41 +233,40 @@
         co[h, pl.ds(2 * u, 2)] = total.reshape(2, 64, WIDTH)
 
     def hop(t, _):
-        @pl.when(t <= 8)
-        def _():
-            for i in (0, 1, 3, 2):
-                @pl.when(t <= 7)
-                def _():
-                    wait(xb.at[0, t, rows(i)], ring_recv.at[0, t, i])
-
-                @pl.when(t <= 6)
-                def _():
-                    pass_up(t, i)
-
-                wait(xb.at[1, t - 1, rows(i)], ring_recv.at[1, t - 1, i])
-
-                @pl.when(t <= 7)
-                def _():
-                    pass_down(t - 1, i)
-
-            select(t - 1)
+        looped = not isinstance(t, int)
+        for i in (0, 1, 3, 2):
+            if looped or t <= 7:
+                wait(xb.at[0, t, rows(i)], ring_recv.at[0, t, i])
+            if looped:
+                pass_up(t, i)
+            wait(xb.at[1, t - 1, rows(i)], ring_recv.at[1, t - 1, i])
+            if looped or t <= 7:
+                pass_down(t - 1, i)
+        select(t - 1)
+        if not looped:
+            gates(t - 2)
+            return 0
 
         @pl.when(t >= 2)
         def _():
             gates(t - 2)
 
-        @pl.when((t >= 5) & (lax.rem(t, 2) == 1))
+        @pl.when(t == 5)
         def _():
-            hidden((t - 5) // 2)
-
-        @pl.when((t >= 7) & (lax.rem(t, 2) == 1))
-        def _():
-            down(t - 7)
-            down(t - 6)
+            hidden(0)
 
         return 0
 
-    lax.fori_loop(1, 10, hop, 0)
+    lax.fori_loop(1, 7, hop, 0)
+    hop(7, 0)
+    hidden(1)
+    down(0)
+    down(1)
+    hop(8, 0)
+    gates(7)
+    hidden(2)
+    down(2)
+    down(3)
     attention()
     hidden(3)
 

time: 104 us -> 104 us (level)
  no operation moved by 1% of the time
where the time goes in v6:
time: 104 us; the launch traced here: 103 us
  Pallas kernels  101 us (97%)
  between operations  1.29 us (1%)
  local copies, waits for them, and re-layouts  1.27 us (1%)
    pallas_call x1, Pallas kernels, per_device(): pl.pallas_call(kernel, out_shape=(jax.ShapeDtypeStruct((TOK, WIDTH), BF16...  101 us

profile of v6, /device:TPU:6, one launch (start us, length us, event | category | flops | bytes accessed | tf_op | source)
XLA Modules:
  0.0 103.5 jit_solution(14197314010658629476)
XLA Ops:
  1.3 100.9 %moe_attention.1 = (bf16[16,896]{1,0:T(8,128)(2,1)S(1)}, bf16[1,128,512]{2,1,0:T(8,128)(2,1)S(1)}) custom-call(bf16[16,896]{1,0:T(8,128)(2,1)} %x_hbm.1, s32[8,16]{1,0:T(8,128)} %bitcast.6, f32[8,16]{1,0:T(8,128)} %bitcast.7, s32[1]{0:T(128)S(6)} %copy.13.len_ref, bf16[1,896,512]{2,1,0:T(8,128)(2,1)} %wg_hbm.1, bf16[1,896,512]{2,1,0:T(8,128)(2,1)} %wu_hbm.1, ...), custom_call_target="tpu_custom_call" | custom-call | tf_op jit(solution)/shard_map/moe_attention/pallas_call | solution.py:362
  102.2 0.6 copy.14
  102.8 0.7 copy.15
